TPU v7x, 256 devices: a whole 4x4x8 slice. The times are simulated.
256 devices in a mesh: inst: 32 (over z, x), head: 8 (over y, core).
Axes of the slice: x: 4, y: 4, z: 8, core: 2. Of those that a mesh axis runs over, the one named last changes fastest.
Arguments:
- latent_cache: bfloat16 [1024, 128, 512], P('inst'), may hold values from -6 to 6
- rope_cache: bfloat16 [1024, 128, 64], P('inst'), may hold values from -6 to 6
- query_nope: bfloat16 [2, 8, 128, 128], P(None, None, 'head'), may hold values from -6 to 6
- query_rope: bfloat16 [2, 8, 128, 64], P(None, None, 'head'), may hold values from -384 to 384
- key_absorb: bfloat16 [128, 128, 512], P('head'), may hold values from -0.5 to 0.5
- value_up_weight: bfloat16 [128, 512, 128], P('head'), may hold values from -0.25 to 0.25
- block_request: int32 [1024], replicated, may hold values from -1 to 7, as said below
- block_index: int32 [1024], replicated, may hold values from 0 to 79, as said below
- request_length: int32 [8], replicated, may hold values from 1 to 10240, as said below
- move_plan: int32 [1024], replicated, may hold values from -1 to 1023, as said below
Outputs:
- attention: float32 [2, 8, 128, 128], P(None, None, 'head')
- moved_latent: bfloat16 [1024, 128, 512], P('inst')
- moved_rope: bfloat16 [1024, 128, 64], P('inst')
Inputs may be any that keep to these rules, and one draw needn't show every extreme that they name: `block_request`: half of the instances retire: each block they hold has a move_plan entry; an instance's blocks fill its first slots; each request's blocks are one run of at least one block in the order of instances and slots. `block_index`: counts blocks from 0 along a request's run; 0 for an empty slot. `request_length`: A request with c blocks has from 128 * (c - 1) + 1 to 128 * c tokens. `move_plan`: targets are empty slots of staying instances, no two alike; at most 2 blocks go from one instance to one other and some pair reaches it; at some staying instance its own and its arriving blocks fill all 32 slots.
All inputs are finite; a program needn't handle non-finite values.
Results may differ from a plain program's by a relative error of at most 0.007.
Values may be sent and summed in bfloat16 or wider, within the bound.
A program may use at most 128 MiB of HBM per device.

v0:
```python
import jax
import jax.numpy as jnp
from jax import lax
from jax.sharding import PartitionSpec as P


def merged(part, axis, combine):
    gathered = jax.tree.map(lambda a: lax.all_gather(a, axis), part)

    def take(source):
        return jax.tree.map(lambda a: lax.dynamic_index_in_dim(a, source, 0, False), gathered)

    return lax.fori_loop(
        1, lax.axis_size(axis), lambda source, state: combine(state, take(source)), take(0)
    )


def combine_partials(first, second):
    row_peak = jnp.maximum(first[0], second[0])
    left_scale = jnp.exp(first[0] - row_peak)
    right_scale = jnp.exp(second[0] - row_peak)
    return (
        row_peak,
        first[1] * left_scale + second[1] * right_scale,
        first[2] * left_scale[:, None] + second[2] * right_scale[:, None],
    )


def attend(
    latent_cache, rope_cache, nope_now, rope_now, key_absorb, owners, offsets, request_length
):
    slot_count, block_length, latent_width = latent_cache.shape
    rope_width = rope_cache.shape[2]
    requests, heads_here, nope_width = nope_now.shape
    absorbed = jnp.einsum(
        "rhn,hnk->rhk", nope_now, key_absorb, preferred_element_type=jnp.float32
    ).astype(jnp.bfloat16)
    latent_query = absorbed.reshape(requests * heads_here, latent_width)
    rope_query = rope_now.reshape(requests * heads_here, rope_width)
    latent_rows = latent_cache.reshape(slot_count * block_length, latent_width)
    rope_rows = rope_cache.reshape(slot_count * block_length, rope_width)
    contract = (((1,), (1,)), ((), ()))
    scores = (
        lax.dot_general(latent_query, latent_rows, contract, preferred_element_type=jnp.float32)
        + lax.dot_general(rope_query, rope_rows, contract, preferred_element_type=jnp.float32)
    ) * (nope_width + rope_width) ** (-0.5)
    within = jnp.arange(block_length, dtype=jnp.int32)
    token_holder = jnp.repeat(owners, block_length)
    token_place = (offsets[:, None] * block_length + within[None, :]).reshape(-1)
    wanted = jnp.arange(requests, dtype=jnp.int32)
    visible = (token_holder[None, :] == wanted[:, None]) & (
        token_place[None, :] < request_length[:, None]
    )
    visible = jnp.broadcast_to(
        visible[:, None, :], (requests, heads_here, slot_count * block_length)
    ).reshape(requests * heads_here, -1)
    scores = jnp.where(visible, scores, -1e30)
    row_peak = jnp.max(scores, axis=1)
    weights = jnp.where(visible, jnp.exp(scores - row_peak[:, None]), 0.0)
    weight_sum = jnp.sum(weights, axis=1)
    summed = jnp.dot(weights.astype(jnp.bfloat16), latent_rows, preferred_element_type=jnp.float32)
    return (row_peak, weight_sum, summed)


def respond(
    latent_cache,
    rope_cache,
    nope_now,
    rope_now,
    key_absorb,
    value_up_weight,
    owners,
    offsets,
    request_length,
):
    requests, heads_here = (nope_now.shape[0], nope_now.shape[1])
    row_peak, weight_sum, summed = attend(
        latent_cache, rope_cache, nope_now, rope_now, key_absorb, owners, offsets, request_length
    )
    latent_width = summed.shape[1]
    row_peak, weight_sum, summed = merged((row_peak, weight_sum, summed), "inst", combine_partials)
    weighted_latent = (
        (summed / weight_sum[:, None])
        .astype(jnp.bfloat16)
        .reshape(requests, heads_here, latent_width)
    )
    return jnp.einsum(
        "wxp,xps->wxs", weighted_latent, value_up_weight, preferred_element_type=jnp.float32
    )


def relocate(latent_cache, rope_cache, block_request, move_plan, myself, devices):
    slot_count, block_length, latent_width = latent_cache.shape
    rope_width = rope_cache.shape[2]
    staying_count = devices // 2
    capacity = -(-slot_count // staying_count)
    owners = lax.dynamic_slice_in_dim(block_request, myself * slot_count, slot_count)
    outgoing = lax.dynamic_slice_in_dim(move_plan, myself * slot_count, slot_count)
    leaving = outgoing >= 0
    target = jnp.where(leaving, outgoing // slot_count, -1)
    slot_ids = jnp.arange(slot_count, dtype=jnp.int32)
    before = slot_ids[None, :] < slot_ids[:, None]
    same_target = (target[None, :] == target[:, None]) & leaving[None, :]
    seat_rank = jnp.sum((before & same_target).astype(jnp.int32), axis=1)
    peer_ids = jnp.arange(devices, dtype=jnp.int32)
    seat_ids = jnp.arange(capacity, dtype=jnp.int32)
    send_table = (
        (
            (target[None, None, :] == peer_ids[:, None, None])
            & (seat_rank[None, None, :] == seat_ids[None, :, None])
            & leaving[None, None, :]
        )
        .astype(jnp.bfloat16)
        .reshape(devices * capacity, slot_count)
    )
    send_latent = (
        jnp.dot(
            send_table,
            latent_cache.reshape(slot_count, block_length * latent_width),
            preferred_element_type=jnp.float32,
        )
        .astype(jnp.bfloat16)
        .reshape(devices, capacity, block_length, latent_width)
    )
    send_rope = (
        jnp.dot(
            send_table,
            rope_cache.reshape(slot_count, block_length * rope_width),
            preferred_element_type=jnp.float32,
        )
        .astype(jnp.bfloat16)
        .reshape(devices, capacity, block_length, rope_width)
    )
    got_latent, got_rope = (
        lax.all_to_all(send_latent, "inst", split_axis=0, concat_axis=0, tiled=True),
        lax.all_to_all(send_rope, "inst", split_axis=0, concat_axis=0, tiled=True),
    )
    whole_plan = move_plan.reshape(devices, slot_count)
    arriving = ((whole_plan >= 0) & (whole_plan // slot_count == myself)).astype(jnp.int32)
    arrival_rank = jnp.cumsum(arriving, axis=1) - arriving
    landing_slot = whole_plan % slot_count
    landing_hit = landing_slot[None, :, :] == slot_ids[:, None, None]
    seat_match = arrival_rank[:, :, None] == seat_ids[None, None, :]
    receive_table = jnp.sum(
        (landing_hit[:, :, :, None] & seat_match[None] & (arriving[None, :, :, None] > 0)).astype(
            jnp.int32
        ),
        axis=2,
    )
    receive_table = receive_table.astype(jnp.bfloat16).reshape(slot_count, devices * capacity)
    landed_latent = (
        jnp.dot(
            receive_table,
            got_latent.reshape(devices * capacity, block_length * latent_width),
            preferred_element_type=jnp.float32,
        )
        .astype(jnp.bfloat16)
        .reshape(slot_count, block_length, latent_width)
    )
    landed_rope = (
        jnp.dot(
            receive_table,
            got_rope.reshape(devices * capacity, block_length * rope_width),
            preferred_element_type=jnp.float32,
        )
        .astype(jnp.bfloat16)
        .reshape(slot_count, block_length, rope_width)
    )
    staying = (owners >= 0) & (outgoing < 0)
    moved_latent = jnp.where(staying[:, None, None], latent_cache, landed_latent)
    moved_rope = jnp.where(staying[:, None, None], rope_cache, landed_rope)
    return (moved_latent, moved_rope)


def shifted_tables(block_request, block_index, move_plan):
    slot_total = block_request.shape[0]
    every_slot = jnp.arange(slot_total, dtype=jnp.int32)
    landing = jnp.where(
        move_plan >= 0, move_plan, jnp.where(block_request >= 0, every_slot, slot_total)
    )
    new_owners = jnp.full((slot_total,), -1, jnp.int32).at[landing].set(block_request, mode="drop")
    new_offsets = jnp.zeros((slot_total,), jnp.int32).at[landing].set(block_index, mode="drop")
    return (new_owners, new_offsets)


def shards(
    latent_cache,
    rope_cache,
    query_nope,
    query_rope,
    key_absorb,
    value_up_weight,
    block_request,
    block_index,
    request_length,
    move_plan,
):
    slot_count = latent_cache.shape[0]
    devices = lax.axis_size("inst")
    myself = lax.axis_index("inst")
    owners = lax.dynamic_slice_in_dim(block_request, myself * slot_count, slot_count)
    offsets = lax.dynamic_slice_in_dim(block_index, myself * slot_count, slot_count)
    decode_outputs = [
        respond(
            latent_cache,
            rope_cache,
            query_nope[0],
            query_rope[0],
            key_absorb,
            value_up_weight,
            owners,
            offsets,
            request_length,
        )
    ]
    moved_latent, moved_rope = relocate(
        latent_cache, rope_cache, block_request, move_plan, myself, devices
    )
    new_owners, new_offsets = shifted_tables(block_request, block_index, move_plan)
    owners_after = lax.dynamic_slice_in_dim(new_owners, myself * slot_count, slot_count)
    offsets_after = lax.dynamic_slice_in_dim(new_offsets, myself * slot_count, slot_count)
    decode_outputs.append(
        respond(
            moved_latent,
            moved_rope,
            query_nope[1],
            query_rope[1],
            key_absorb,
            value_up_weight,
            owners_after,
            offsets_after,
            request_length,
        )
    )
    return (jnp.stack(decode_outputs), moved_latent, moved_rope)


def solution(mesh):
    return jax.shard_map(
        shards,
        mesh=mesh,
        in_specs=(
            P("inst", None, None),
            P("inst", None, None),
            P(None, None, "head", None),
            P(None, None, "head", None),
            P("head", None, None),
            P("head", None, None),
            P(),
            P(),
            P(),
            P(),
        ),
        out_specs=(P(None, None, "head", None), P("inst", None, None), P("inst", None, None)),
        check_vma=False,
    )
```

profile of v0, /device:TPU:8, one launch (start us, length us, event | category | flops | bytes accessed | tf_op | source)
XLA Modules:
  0.0 564.6 jit_solution(9109300636424424307)
XLA Ops:
  8.8 4.5 scatter_custom_fusion.1
  14.3 1.5 copy.58
  15.9 1.6 reshape.453
  17.5 2.4 convolution_convert_fusion.2
  19.9 4.2 reshape.454
  24.2 2.7 copy.56
  26.9 11.4 %all-to-all-start.1 = ((bf16[32,2,128,64]{2,3,1,0:T(8,128)(2,1)}), bf16[32,2,128,64]{2,3,1,0:T(8,128)(2,1)}, u32[]{:S(2)}, u32[]{:S(2)}) async-start(bf16[32,2,128,64]{2,3,1,0:T(8,128)(2,1)} %copy.56), calls=%async_computation.1 | async-start | bytes 2097152 | tf_op jit(solution)/shard_map/all_to_all | solution.py:136
  38.3 4.7 scatter_custom_fusion
  43.5 4.6 copy.69
  48.1 5.5 convolution_convert_fusion
  53.6 9.9 %copy.70 = bf16[8,8,128,512]{3,2,1,0:T(8,128)(2,1)} copy(bf16[8,8,128,512]{3,1,2,0:T(8,128)(2,1)} %bitcast.169) | data formatting | bytes 16777216
  64.5 1.9 all-to-all-done.1
  66.4 7.9 %all-to-all-start = ((bf16[32,2,128,512]{3,2,1,0:T(8,128)(2,1)}), bf16[32,2,128,512]{3,2,1,0:T(8,128)(2,1)}, u32[]{:S(2)}, u32[]{:S(2)}) async-start(bf16[32,2,128,512]{3,2,1,0:T(8,128)(2,1)} %bitcast.168), calls=%async_computation | async-start | bytes 16777216 | tf_op jit(solution)/shard_map/all_to_all | solution.py:135
  74.4 3.7 fusion.44
  80.7 1.4 fusion.45
  82.8 1.2 convert_reduce_fusion
  84.6 2.0 copy.57
  86.6 2.5 reshape.455
  89.1 1.6 convolution_convert_fusion.3
  90.7 1.1 reshape.456
  92.0 213.9 %all-to-all-done = bf16[32,2,128,512]{3,2,1,0:T(8,128)(2,1)} async-done(((bf16[32,2,128,512]{3,2,1,0:T(8,128)(2,1)}), bf16[32,2,128,512]{3,2,1,0:T(8,128)(2,1)}, u32[]{:S(2)}, u32[]{:S(2)}) %all-to-all-start) | async-done | bytes 8388640 | tf_op jit(solution)/shard_map/all_to_all | solution.py:135
  305.9 11.8 %copy.71 = bf16[8,8,128,512]{3,1,2,0:T(8,128)(2,1)} copy(bf16[8,8,128,512]{3,2,1,0:T(8,128)(2,1)} %bitcast.55) | data formatting | bytes 16777216
  317.6 4.7 convolution_convert_fusion.1
  322.3 1.5 copy.72
  325.5 1.5 fusion.46
  328.6 1.5 fusion.47
  330.1 39.1 %all-gather.7 = f32[32,1,128]{2,1,0:T(1,128)S(1)} all-gather(f32[1,1,128]{2,1,0:T(1,128)S(1)} %bitcast.192), channel_id=3, replica_groups=mesh['inst'=32,'head'=8] {'inst'}, dimensions={0}, use_global_device_ids=true | all-gather | bytes 16896 | tf_op jit(solution)/shard_map/all_gather | solution.py:8
  369.2 38.1 %all-gather.6 = f32[32,1,128]{2,1,0:T(1,128)S(1)} all-gather(f32[1,1,128]{2,1,0:T(1,128)S(1)} %bitcast.191), channel_id=2, replica_groups=mesh['inst'=32,'head'=8] {'inst'}, dimensions={0}, use_global_device_ids=true | all-gather | bytes 16896 | tf_op jit(solution)/shard_map/all_gather | solution.py:8
  407.4 1.1 copy.63
  409.5 35.6 %all-gather.9 = f32[32,1,128]{2,1,0:T(1,128)S(1)} all-gather(f32[1,1,128]{2,1,0:T(1,128)S(1)} %bitcast.193), channel_id=6, replica_groups=mesh['inst'=32,'head'=8] {'inst'}, dimensions={0}, use_global_device_ids=true | all-gather | bytes 16896 | tf_op jit(solution)/shard_map/all_gather | solution.py:8
  445.0 36.9 %all-gather.8 = f32[32,1,128]{2,1,0:T(1,128)S(1)} all-gather(f32[1,1,128]{2,1,0:T(1,128)S(1)} %bitcast.190), channel_id=5, replica_groups=mesh['inst'=32,'head'=8] {'inst'}, dimensions={0}, use_global_device_ids=true | all-gather | bytes 16896 | tf_op jit(solution)/shard_map/all_gather | solution.py:8
  481.9 34.9 %while.38 = (s32[]{:T(128)}, f32[128]{0:T(128)S(1)}, f32[128]{0:T(128)S(1)}, f32[128,512]{1,0:T(8,128)S(1)}, f32[32,128]{1,0:T(8,128)S(1)}, /*index=5*/f32[32,12...) while((s32[]{:T(128)}, f32[128]{0:T(128)S(1)}, f32[128]{0:T(128)S(1)}, ...), condition=%wide.region_3.4_spmd, body=%wide.region_2.3_spmd.sunk | while | flops 197381 | bytes 791703 | solution.py:13
  486.5 1.1 fusion.77
  487.6 1.1 fusion.77
  493.2 1.1 fusion.77
  494.3 1.1 fusion.77
  495.5 1.1 fusion.77
  501.1 1.1 fusion.77
  502.2 1.1 fusion.77
  507.8 1.1 fusion.77
  509.0 1.1 fusion.77
  514.6 1.1 fusion.77
  515.7 1.1 fusion.77
  516.9 2.0 convolution_bitcast_fusion.2
  519.9 34.9 %while.39 = (s32[]{:T(128)}, f32[128]{0:T(128)S(1)}, f32[128]{0:T(128)S(1)}, f32[128,512]{1,0:T(8,128)S(1)}, f32[32,128]{1,0:T(8,128)S(1)}, /*index=5*/f32[32,12...) while((s32[]{:T(128)}, f32[128]{0:T(128)S(1)}, f32[128]{0:T(128)S(1)}, ...), condition=%wide.region_12.13_spmd, body=%wide.region_11.12_spmd.sunk | while | flops 197381 | bytes 791703 | solution.py:13
  520.0 1.1 fusion.79
  525.6 1.1 fusion.79
  554.9 2.1 convolution_bitcast_fusion.1
  (184 shorter events, 68.3 us)
Async XLA Ops:
  7.2 35.9 %copy-start = (bf16[16,128,512]{2,1,0:T(8,128)(2,1)S(1)}, bf16[16,128,512]{2,1,0:T(8,128)(2,1)}, u32[]{:S(2)}) copy-start(bf16[16,128,512]{2,1,0:T(8,128)(2,1)} %param.18) | copy-start | bytes 6291460
  24.2 18.9 %copy-start.6 = (bf16[2,8,16,128]{3,2,1,0:T(8,128)(2,1)S(1)}, bf16[2,8,16,128]{3,2,1,0:T(8,128)(2,1)}, u32[]{:S(2)}) copy-start(bf16[2,8,16,128]{3,2,1,0:T(8,128)(2,1)} %param.16) | copy-start | bytes 196612
  26.9 39.5 %all-to-all-start.1 = ((bf16[32,2,128,64]{2,3,1,0:T(8,128)(2,1)}), bf16[32,2,128,64]{2,3,1,0:T(8,128)(2,1)}, u32[]{:S(2)}, u32[]{:S(2)}) async-start(bf16[32,2,128,64]{2,3,1,0:T(8,128)(2,1)} %copy.56), calls=%async_computation.1 | async-start | bytes 2097152 | tf_op jit(solution)/shard_map/all_to_all | solution.py:136
  53.6 10.8 %copy-start.7 = (bf16[2,8,16,64]{3,2,1,0:T(8,128)(2,1)S(1)}, bf16[2,8,16,64]{3,2,1,0:T(8,128)(2,1)}, u32[]{:S(2)}) copy-start(bf16[2,8,16,64]{3,2,1,0:T(8,128)(2,1)} %param.17) | copy-start | bytes 98308
  66.4 239.5 %all-to-all-start = ((bf16[32,2,128,512]{3,2,1,0:T(8,128)(2,1)}), bf16[32,2,128,512]{3,2,1,0:T(8,128)(2,1)}, u32[]{:S(2)}, u32[]{:S(2)}) async-start(bf16[32,2,128,512]{3,2,1,0:T(8,128)(2,1)} %bitcast.168), calls=%async_computation | async-start | bytes 16777216 | tf_op jit(solution)/shard_map/all_to_all | solution.py:135
  74.3 334.2 %all-gather.13.cloned.1.call-start = ((), (), s32[]{:S(2)}) async-start(), calls=%async_computation.2 | async-start | bytes 8650752 | tf_op jit(solution)/shard_map/all_gather | solution.py:8
  74.4 3.7 copy-start.9
  74.4 4.1 copy-start.5
  78.5 2.2 copy-start.2
  80.7 1.7 copy-start.8
  82.1 436.8 %all-gather.15.cloned.1.call-start = ((), (), s32[]{:S(2)}) async-start(), calls=%async_computation.3 | async-start | bytes 8650752 | tf_op jit(solution)/shard_map/all_gather | solution.py:8
  322.3 2.2 copy-start.3
  325.5 3.1 copy-start.4
  554.8 3.0 copy-start.1
Sparse Core Ops, SparseCore 0:
  82.3 212.6 all-gather.12
  330.3 98.0 all-gather.14
where the time goes:
time: 568 us; the launch traced here: 565 us
  waiting for transfers between devices  216 us (38%)
  blocking collectives  150 us (26%)
  other arithmetic  75.9 us (13%)
  local copies, waits for them, and re-layouts  58.7 us (10%)
  matrix products  28.6 us (5%)
  starting transfers between devices  19.7 us (3%)
  between operations  14.4 us (3%)
    all_to_all x1, waiting for transfers between devices, relocate(): lax.all_to_all(send_latent, 'inst', split_axis=0, concat_axis=0, tiled=True)  214 us
    all_gather x4, blocking collectives, merged(): gathered = jax.tree.map(lambda a: lax.all_gather(a, axis), part)  150 us
    add x62, other arithmetic, combine_partials(): first[2] * left_scale[:, None] + second[2] * right_scale[:, None]  66.3 us
    unnamed x27, local copies, waits for them, and re-layouts  32.6 us
    all_to_all x1, starting transfers between devices, relocate(): lax.all_to_all(send_rope, 'inst', split_axis=0, concat_axis=0, tiled=True)  11.4 us
  transfers between devices with their start and end apart: 4, of which 2 were waited for; matrix products, arithmetic and copies ran while one was open for 18% of the time, Pallas kernels for 0%

commit v1 on v0

v1 whole, which is shorter than its diff:
```python
import functools

import jax
import jax.numpy as jnp
from jax import lax
from jax.experimental import pallas as pl
from jax.experimental.pallas import tpu as pltpu
from jax.sharding import PartitionSpec as P

MESH = pl.DeviceIdType.MESH
HIDDEN = -1e30
FLOOR = -1e29
TILE = 128
ROWS = 16
LANE_TILES = ((0, 1), (2, 3))
ROPE_CHUNK = 1
NEG = -1


def kernel(
    lat_hbm,
    rope_hbm,
    nope_hbm,
    qrope_hbm,
    absorb_hbm,
    value_hbm,
    owner_hbm,
    index_hbm,
    length_hbm,
    plan_hbm,
    out_att,
    out_lat,
    out_rope,
    lat_vm,
    rope_vm,
    nope_vm,
    qrope_vm,
    absorb_vm,
    value_vm,
    plan_vm,
    owner_sm,
    index_sm,
    length_sm,
    table_vm,
    table_sm,
    share,
    rope_share,
    landed,
    landed_rope,
    rope_got,
    query,
    scores,
    att_send,
    att_got,
    att_all,
    send0,
    send1,
    got0,
    got1,
    in_sem,
    a2a_send,
    a2a_recv,
    att_sem,
    own_sem,
    ag_send,
    ag_recv,
):
    insts = lax.axis_size("inst")
    me = lax.axis_index("inst")
    head = lax.axis_index("head")
    core = lax.rem(head, 2)
    y = head // 2
    up = lax.rem(y + 1, 4)
    down = lax.rem(y + 3, 4)
    far = lax.rem(y + 2, 4)
    other = 1 - core
    slots = lat_vm.shape[0]
    sends, gots = (send0, send1), (got0, got1)
    parts = len(LANE_TILES)

    def fetch(k, source, target):
        copy = pltpu.make_async_copy(source, target, in_sem.at[k])
        copy.start()
        return copy

    rows = pl.ds(pl.multiple_of(head * ROWS, ROWS), ROWS)
    get_plan = fetch(0, plan_hbm, plan_vm)
    get_share = fetch(1, lat_hbm.at[:, rows, :], share)
    get_rope = fetch(2, rope_hbm, rope_vm)
    get_owner = fetch(3, owner_hbm, owner_sm)
    get_index = fetch(4, index_hbm, index_sm)
    get_length = fetch(5, length_hbm, length_sm)
    get_nope = fetch(6, nope_hbm, nope_vm)
    get_absorb = fetch(7, absorb_hbm, absorb_vm)
    get_qrope = fetch(8, qrope_hbm, qrope_vm)
    get_lat = fetch(9, lat_hbm, lat_vm)
    get_value = fetch(10, value_hbm, value_vm)

    barrier = pltpu.get_barrier_semaphore()

    def greet(k, carry):
        pl.semaphore_signal(
            barrier,
            inc=1,
            device_id={"inst": lax.rem(me + k, insts)},
            device_id_type=MESH,
        )
        return carry

    lax.fori_loop(1, insts, greet, 0)
    mates = (y * 2 + other, up * 2 + core, down * 2 + core)
    for mate in mates:
        pl.semaphore_signal(barrier, inc=1, device_id={"head": mate}, device_id_type=MESH)

    get_plan.wait()
    plan = plan_vm[...]
    lane = lax.broadcasted_iota(jnp.int32, (8, TILE), 1)
    row = lax.broadcasted_iota(jnp.int32, (8, TILE), 0)
    per_row = TILE // slots
    group = lane // slots
    within = lane - group * slots
    seen = jnp.where((plan >> 5) == me, 1, 0)
    for d in (1, 2, 4, 8, 16):
        seen = jnp.maximum(seen, jnp.where(within >= d, pltpu.roll(seen, d, 1), 0))
    rank = jnp.where(within >= 1, pltpu.roll(seen, 1, 1), 0)
    code = (row * per_row + group) * 2 + rank
    column = lax.broadcasted_iota(jnp.int32, (slots, TILE), 0)
    lanes = lax.broadcasted_iota(jnp.int32, (slots, TILE), 1)
    hit = jnp.full((slots, TILE), NEG, jnp.int32)
    for r in range(8):
        wanted = jnp.broadcast_to(plan[r : r + 1, :], (slots, TILE)) == me * slots + column
        hit = jnp.maximum(
            hit, jnp.where(wanted, jnp.broadcast_to(code[r : r + 1, :], (slots, TILE)), NEG)
        )
    land = jnp.max(hit, axis=1, keepdims=True)
    mine = plan_vm[pl.ds(me // per_row, 1), :]
    own_lane = lax.rem(me, per_row) * slots + column
    own = jnp.max(
        jnp.where(lanes == own_lane, jnp.broadcast_to(mine, (slots, TILE)), NEG),
        axis=1,
        keepdims=True,
    )
    mine = jnp.where(group[:1] == lax.rem(me, per_row), mine >> 5, NEG)
    goes = jnp.broadcast_to(mine, (slots, TILE)) == column
    place = lanes - lanes // slots * slots
    first = jnp.min(jnp.where(goes, place, slots), axis=1, keepdims=True)
    last = jnp.max(jnp.where(goes, place, 0), axis=1, keepdims=True)
    first = jnp.where(first >= slots, 0, first)
    table_vm[...] = jnp.where(
        lanes == 0,
        jnp.broadcast_to(first, (slots, TILE)),
        jnp.where(
            lanes == 1,
            jnp.broadcast_to(last, (slots, TILE)),
            jnp.where(
                lanes == 2,
                jnp.broadcast_to(land, (slots, TILE)),
                jnp.broadcast_to(own, (slots, TILE)),
            ),
        ),
    )
    get_table = fetch(11, table_vm, table_sm)

    get_rope.wait()
    half = pl.ds(pl.multiple_of(y * ROWS, ROWS), ROWS)

    def cut_rope(t, carry):
        piece = rope_vm[t, half, :].astype(jnp.float32)
        rope_share[t] = jnp.where(core == 0, piece[:8], piece[8:])
        return carry

    lax.fori_loop(0, slots, cut_rope, 0, unroll=4)
    get_share.wait()
    get_table.wait()
    get_owner.wait()
    get_index.wait()
    get_length.wait()

    for part in range(parts):
        tiles = LANE_TILES[part]
        count = len(tiles)
        buffer = sends[part]

        def pack(j, carry, tiles=tiles, count=count, buffer=buffer, part=part):
            picks = (table_sm[j, 0], table_sm[j, 1])
            for seat in range(2):
                for n, tile in enumerate(tiles):
                    buffer[j, seat * count + n] = share[
                        picks[seat], :, tile * TILE : (tile + 1) * TILE
                    ]
            if part == ROPE_CHUNK:
                buffer[j, 2 * count] = jnp.concatenate(
                    [rope_share[picks[0]], rope_share[picks[1]]], axis=0
                ).astype(jnp.bfloat16)
            return carry

        lax.fori_loop(0, insts, pack, 0, unroll=4)
        if part == 0:
            pl.semaphore_wait(barrier, insts - 1 + len(mates))

        def ship(k, carry, part=part, buffer=buffer):
            peer = lax.rem(me + k, insts)
            pltpu.make_async_remote_copy(
                src_ref=buffer.at[peer],
                dst_ref=gots[part].at[me],
                send_sem=a2a_send.at[part],
                recv_sem=a2a_recv.at[part],
                device_id={"inst": peer},
                device_id_type=MESH,
            ).start()
            return carry

        lax.fori_loop(1, insts, ship, 0)

    heads = 16
    queries = nope_vm.shape[0]
    row_head = lax.rem(lax.broadcasted_iota(jnp.int32, (queries, 1), 0), heads)
    row_request = lax.rem(lax.broadcasted_iota(jnp.int32, (queries, 1), 0) // heads, 8)
    get_nope.wait()
    get_absorb.wait()
    width = lat_vm.shape[2]

    def absorb(h, total):
        part_query = jnp.where(row_head == h, nope_vm[...], jnp.zeros((), jnp.bfloat16))
        return total + jnp.dot(part_query, absorb_vm[h], preferred_element_type=jnp.float32)

    absorbed = lax.fori_loop(0, heads, absorb, jnp.zeros((queries, width), jnp.float32))
    query[...] = absorbed.astype(jnp.bfloat16)
    get_qrope.wait()
    get_lat.wait()
    scale = 192.0**-0.5
    pair = 2 * TILE
    lane_row = lax.broadcasted_iota(jnp.int32, (1, TILE), 1)

    def score(i, peak):
        block = lat_vm[pl.ds(2 * i, 2)].reshape(pair, width)
        raw = lax.dot_general(
            query[...], block, (((1,), (1,)), ((), ())), preferred_element_type=jnp.float32
        )
        turned = []
        holders = []
        for b in range(2):
            turned.append(
                jnp.dot(qrope_vm[...], rope_vm[2 * i + b], preferred_element_type=jnp.float32)
            )
            g = lax.rem(me, per_row) * slots + 2 * i + b
            owner = owner_sm[me // per_row, g]
            left = length_sm[jnp.maximum(owner, 0)] - index_sm[me // per_row, g] * TILE
            holders.append(jnp.where(lane_row < left, owner, NEG))
        raw = (raw + jnp.concatenate(turned, axis=1)) * scale
        raw = jnp.where(jnp.concatenate(holders, axis=1) == row_request, raw, HIDDEN)
        scores[i] = raw
        return jnp.maximum(peak, raw)

    peak = lax.fori_loop(
        0, slots // 2, score, jnp.full((queries, pair), FLOOR, jnp.float32)
    )
    peak = jnp.max(peak, axis=1, keepdims=True)

    def weigh(i, carry):
        total, summed = carry
        weights = jnp.exp(scores[i] - peak)
        block = lat_vm[pl.ds(2 * i, 2)].reshape(pair, width)
        summed = summed + jnp.dot(
            weights.astype(jnp.bfloat16), block, preferred_element_type=jnp.float32
        )
        return total + weights, summed

    total, summed = lax.fori_loop(
        0,
        slots // 2,
        weigh,
        (jnp.zeros((queries, pair), jnp.float32), jnp.zeros((queries, width), jnp.float32)),
    )
    total = jnp.sum(total, axis=1, keepdims=True)
    query[...] = summed.astype(jnp.bfloat16)
    get_value.wait()

    def project(n, result):
        both = jnp.concatenate([value_vm[2 * n], value_vm[2 * n + 1]], axis=1)
        got = jnp.dot(query[...], both, preferred_element_type=jnp.float32)
        result = jnp.where(row_head == 2 * n, got[:, :TILE], result)
        return jnp.where(row_head == 2 * n + 1, got[:, TILE:], result)

    projected = lax.fori_loop(
        0, heads // 2, project, jnp.zeros((queries, TILE), jnp.float32)
    )
    wide = lax.broadcasted_iota(jnp.int32, (queries, TILE), 1)
    stats = jnp.where(
        wide < TILE // 2,
        jnp.broadcast_to(peak, (queries, TILE)),
        jnp.broadcast_to(total, (queries, TILE)),
    )
    att_send[:, 0] = projected.reshape(insts, 8, TILE)
    att_send[:, 1] = stats.reshape(insts, 8, TILE)
    att_got[me] = att_send[me]

    def ship_partial(k, carry):
        peer = lax.rem(me + k, insts)
        pltpu.make_async_remote_copy(
            src_ref=att_send.at[peer],
            dst_ref=att_got.at[me],
            send_sem=att_sem.at[0],
            recv_sem=att_sem.at[1],
            device_id={"inst": peer},
            device_id_type=MESH,
        ).start()
        return carry

    lax.fori_loop(1, insts, ship_partial, 0)

    def wait_all(buffer, sem):
        whole = buffer.at[pl.ds(0, insts - 1)]
        pltpu.make_async_copy(whole, whole, sem).wait()

    def region(unit, h, which):
        n = slots if unit < parts else slots // 2
        span = {
            None: pl.ds(0, n),
            0: pl.ds(0, n // 2),
            1: pl.ds(n // 2, n // 2),
        }[which]
        if unit < parts:
            tiles = LANE_TILES[unit]
            return out_lat.at[
                span,
                pl.ds(pl.multiple_of(h * ROWS, ROWS), ROWS),
                pl.ds(tiles[0] * TILE, len(tiles) * TILE),
            ]
        return out_rope.at[h, span]

    def own_region(unit):
        if unit < parts:
            tiles = LANE_TILES[unit]
            return landed.at[:, :, pl.ds(tiles[0] * TILE, len(tiles) * TILE)]
        return landed_rope

    started = []

    def send(unit, k, source, h, which, mate):
        copy = pltpu.make_async_remote_copy(
            src_ref=source,
            dst_ref=region(unit, h, which),
            send_sem=ag_send.at[unit, k],
            recv_sem=ag_recv.at[unit, k],
            device_id={"head": mate},
            device_id_type=MESH,
        )
        copy.start()
        started.append(copy)

    def arrived(unit, k, h, which):
        here = region(unit, h, which)
        pltpu.make_async_copy(here, here, ag_recv.at[unit, k]).wait()

    side, above, below = mates
    h_up, h_down, h_far = up * 2 + core, down * 2 + core, far * 2 + core
    o_up, o_down, o_far = up * 2 + other, down * 2 + other, far * 2 + other
    keeping = []

    def place_part(part):
        tiles = LANE_TILES[part]
        count = len(tiles)
        buffer = gots[part]
        wait_all(buffer, a2a_recv.at[part])

        def put(t, carry):
            where = table_sm[t, 2]
            g = lax.rem(me, per_row) * slots + t
            keep = (owner_sm[me // per_row, g] >= 0) & (table_sm[t, 3] < 0)
            spot = jnp.maximum(where, 0)
            source, seat = spot // 2, lax.rem(spot, 2)
            for n, tile in enumerate(tiles):
                span = slice(tile * TILE, (tile + 1) * TILE)
                moved = buffer[source, seat * count + n]
                kept = share[t, :, span]
                zero = jnp.zeros_like(moved)
                landed[t, :, span] = jnp.where(
                    keep, kept, jnp.where(where >= 0, moved, zero)
                )
            if part == ROPE_CHUNK:
                pieces = buffer[source, 2 * count].astype(jnp.float32)
                moved = jnp.where(seat == 0, pieces[:8], pieces[8:])
                zero = jnp.zeros_like(moved)
                rope_got[t] = jnp.where(
                    keep, rope_share[t], jnp.where(where >= 0, moved, zero)
                )
            return carry

        lax.fori_loop(0, slots, put, 0, unroll=4)
        units = [part]
        if part == ROPE_CHUNK:
            landed_rope[...] = (
                rope_got[...].reshape(slots // 2, ROWS, TILE).astype(jnp.bfloat16)
            )
            units.append(parts)
        for unit in units:
            source = own_region(unit)
            copy = pltpu.make_async_copy(source, region(unit, head, None), own_sem.at[unit])
            copy.start()
            keeping.append(copy)
            send(unit, 1, source, head, None, above)
            send(unit, 2, source, head, None, below)
            send(unit, 0, source, head, None, side)

    def relay(unit):
        arrived(unit, 1, h_down, None)
        send(unit, 5, region(unit, h_down, 0), h_down, 0, above)
        send(unit, 3, region(unit, h_down, None), h_down, None, side)
        arrived(unit, 2, h_up, None)
        send(unit, 6, region(unit, h_up, 1), h_up, 1, below)
        send(unit, 4, region(unit, h_up, None), h_up, None, side)

    def finish(unit):
        arrived(unit, 5, h_far, 0)
        send(unit, 7, region(unit, h_far, 0), h_far, 0, side)
        arrived(unit, 6, h_far, 1)
        send(unit, 8, region(unit, h_far, 1), h_far, 1, side)

    def combine():
        wait_all(att_got, att_sem.at[1])
        got = att_got[...]
        partial, stat = got[:, 0], got[:, 1]
        peaks, totals = stat[:, :, :1], stat[:, :, TILE // 2 : TILE // 2 + 1]
        top = jnp.max(peaks, axis=0, keepdims=True)
        weight = jnp.exp(peaks - top)
        above_line = jnp.sum(partial * weight, axis=0)
        below_line = jnp.sum(totals * weight, axis=0)
        att_all[me] = above_line / below_line

        def ship_result(k, carry):
            pltpu.make_async_remote_copy(
                src_ref=att_all.at[me],
                dst_ref=att_all.at[me],
                send_sem=att_sem.at[2],
                recv_sem=att_sem.at[3],
                device_id={"inst": lax.rem(me + k, insts)},
                device_id_type=MESH,
            ).start()
            return carry

        lax.fori_loop(1, insts, ship_result, 0)

    place_part(0)
    combine()
    place_part(1)
    relay(0)
    relay(1)
    relay(2)
    finish(0)
    finish(1)
    finish(2)

    wait_all(att_all, att_sem.at[3])
    out_att[...] = att_all[...].reshape(queries, TILE)
    for unit in range(parts + 1):
        arrived(unit, 0, y * 2 + other, None)
        arrived(unit, 3, o_down, None)
        arrived(unit, 4, o_up, None)
        arrived(unit, 7, o_far, 0)
        arrived(unit, 8, o_far, 1)
    for copy in keeping:
        copy.wait()
    for copy in started:
        copy.wait_send()
    for part in range(parts):
        wait_all(sends[part], a2a_send.at[part])
    wait_all(att_send, att_sem.at[0])
    wait_all(att_all, att_sem.at[2])


def shards(
    latent_cache,
    rope_cache,
    query_nope,
    query_rope,
    key_absorb,
    value_up_weight,
    block_request,
    block_index,
    request_length,
    move_plan,
):
    slots, block, width = latent_cache.shape
    rope_width = rope_cache.shape[2]
    steps, requests, heads, nope_width = query_nope.shape
    queries = steps * requests * heads
    insts = lax.axis_size("inst")
    heads_axis = lax.axis_size("head")
    bf16, f32, i32 = jnp.bfloat16, jnp.float32, jnp.int32
    tiles = [
        2 * len(LANE_TILES[p]) + (1 if p == ROPE_CHUNK else 0) for p in range(len(LANE_TILES))
    ]
    units = len(LANE_TILES) + 1
    anywhere = pl.BlockSpec(memory_space=pl.ANY)
    attention, moved, rope = pl.pallas_call(
        kernel,
        out_shape=(
            jax.ShapeDtypeStruct((queries, TILE), f32),
            jax.ShapeDtypeStruct(latent_cache.shape, bf16),
            jax.ShapeDtypeStruct((heads_axis, slots // 2, ROWS, TILE), bf16),
        ),
        in_specs=[anywhere] * 10,
        out_specs=(pl.BlockSpec(memory_space=pltpu.VMEM), anywhere, anywhere),
        scratch_shapes=[
            pltpu.VMEM((slots, block, width), bf16),
            pltpu.VMEM((slots, rope_width, block), bf16),
            pltpu.VMEM((queries, nope_width), bf16),
            pltpu.VMEM((queries, rope_width), bf16),
            pltpu.VMEM(key_absorb.shape, bf16),
            pltpu.VMEM(value_up_weight.shape, bf16),
            pltpu.VMEM((8, TILE), i32),
            pltpu.SMEM((8, TILE), i32),
            pltpu.SMEM((8, TILE), i32),
            pltpu.SMEM((8,), i32),
            pltpu.VMEM((slots, TILE), i32),
            pltpu.SMEM((slots, TILE), i32),
            pltpu.VMEM((slots, ROWS, width), bf16),
            pltpu.VMEM((slots, 8, TILE), f32),
            pltpu.VMEM((slots, ROWS, width), bf16),
            pltpu.VMEM((slots // 2, ROWS, TILE), bf16),
            pltpu.VMEM((slots, 8, TILE), f32),
            pltpu.VMEM((queries, width), bf16),
            pltpu.VMEM((slots // 2, queries, 2 * TILE), f32),
            pltpu.VMEM((insts, 2, 8, TILE), f32),
            pltpu.VMEM((insts, 2, 8, TILE), f32),
            pltpu.VMEM((insts, 8, TILE), f32),
        ]
        + [pltpu.VMEM((insts, n, ROWS, TILE), bf16) for n in tiles]
        + [pltpu.VMEM((insts, n, ROWS, TILE), bf16) for n in tiles]
        + [
            pltpu.SemaphoreType.DMA((12,)),
            pltpu.SemaphoreType.DMA((len(tiles),)),
            pltpu.SemaphoreType.DMA((len(tiles),)),
            pltpu.SemaphoreType.DMA((4,)),
            pltpu.SemaphoreType.DMA((units,)),
            pltpu.SemaphoreType.DMA((units, 9)),
            pltpu.SemaphoreType.DMA((units, 9)),
        ],
        compiler_params=pltpu.CompilerParams(
            collective_id=0, has_side_effects=True, vmem_limit_bytes=56 * 2**20
        ),
        name="decode_and_move",
    )(
        latent_cache,
        rope_cache.swapaxes(1, 2),
        query_nope.reshape(queries, nope_width),
        query_rope.reshape(queries, rope_width),
        key_absorb,
        value_up_weight,
        block_request.reshape(8, TILE),
        block_index.reshape(8, TILE),
        request_length,
        move_plan.reshape(8, TILE),
    )
    rope = rope.reshape(heads_axis, slots, 8, TILE).swapaxes(0, 1)
    rope = rope.reshape(slots, rope_width, block).swapaxes(1, 2)
    return attention.reshape(steps, requests, heads, TILE), moved, rope


def solution(mesh):
    return jax.shard_map(
        shards,
        mesh=mesh,
        in_specs=(
            P("inst", None, None),
            P("inst", None, None),
            P(None, None, "head", None),
            P(None, None, "head", None),
            P("head", None, None),
            P("head", None, None),
            P(),
            P(),
            P(),
            P(),
        ),
        out_specs=(P(None, None, "head", None), P("inst", None, None), P("inst", None, None)),
        check_vma=False,
    )
```

time: 568 us -> 72.7 us (0.13)
  the two profiles are of different devices: /device:TPU:8 before, /device:TPU:1 now
where the time goes in v1:
time: 72.7 us; the launch traced here: 72.5 us
  Pallas kernels  63.7 us (88%)
  local copies, waits for them, and re-layouts  8.18 us (11%)
    pallas_call x1, Pallas kernels, shards(): pl.pallas_call(kernel, out_shape=(jax.ShapeDtypeStruct((queries, TILE), f...  63.7 us
    unnamed x2, local copies, waits for them, and re-layouts  6.2 us
    transpose x1, local copies, waits for them, and re-layouts, shards(): rope = rope.reshape(heads_axis, slots, 8, TILE).swapaxes(0, 1)  1.98 us

profile of v1, /device:TPU:1, one launch (start us, length us, event | category | flops | bytes accessed | tf_op | source)
XLA Modules:
  0.0 72.5 jit_solution(18411668539421342296)
XLA Ops:
  0.6 63.7 %decode_and_move.1 = (f32[256,128]{1,0:T(8,128)}, bf16[32,128,512]{2,1,0:T(8,128)(2,1)}, bf16[8,16,16,128]{3,2,1,0:T(8,128)(2,1)}) custom-call(bf16[32,128,512]{2,1,0:T(8,128)(2,1)} %lat_hbm.1, bf16[32,64,128]{2,1,0:T(8,128)(2,1)} %bitcast.15, bf16[256,128]{1,0:T(8,128)(2,1)} %bitcast.19, bf16[256,64]{1,0:T(8,128)(2,1)} %bitcast.20, ...), custom_call_target="tpu_custom_call" | custom-call | tf_op jit(solution)/shard_map/decode_and_move/pallas_call | solution.py:496
  64.3 2.0 %copy.15 = bf16[32,8,8,128]{3,2,1,0:T(8,128)(2,1)} copy(bf16[32,8,8,128]{3,2,0,1:T(8,128)(2,1)} %bitcast.17) | data formatting | bytes 1048576 | tf_op jit(solution)/shard_map/transpose | solution.py:556
  66.3 1.6 %copy.18 = f32[2,8,16,128]{3,2,1,0:T(8,128)} copy(f32[2,8,16,128]{3,2,1,0:T(8,128)} %bitcast.18) | data formatting | bytes 262144
  67.9 4.6 %copy.19 = bf16[32,128,512]{2,1,0:T(8,128)(2,1)} copy(bf16[32,128,512]{2,1,0:T(8,128)(2,1)} %get-tuple-element.13) | data formatting | bytes 8388608

commit v2 on v1

--- a/solution.py
+++ b/solution.py
@@ -12,8 +12,9 @@
 FLOOR = -1e29
 TILE = 128
 ROWS = 16
-LANE_TILES = ((0, 1), (2, 3))
-ROPE_CHUNK = 1
+LANE_TILES = ((0,), (1,), (2,), (3,))
+ROPE_CHUNK = 0
+Z, X = 8, 4
 NEG = -1
 
 
@@ -45,26 +46,21 @@
     table_sm,
     share,
     rope_share,
-    landed,
-    landed_rope,
     rope_got,
     query,
     scores,
-    att_send,
-    att_got,
-    att_all,
-    send0,
-    send1,
-    got0,
-    got1,
-    in_sem,
-    a2a_send,
-    a2a_recv,
-    att_sem,
-    own_sem,
-    ag_send,
-    ag_recv,
+    x_send,
+    x_got,
+    z_send,
+    z_got,
+    z_all,
+    x_all,
+    *rest,
+
 ):
+    parts = len(LANE_TILES)
+    sends, gots = rest[:parts], rest[parts : 2 * parts]
+    in_sem, a2a_send, a2a_recv, att_sem, ag_send, ag_recv = rest[2 * parts :]
     insts = lax.axis_size("inst")
     me = lax.axis_index("inst")
     head = lax.axis_index("head")
@@ -75,8 +71,7 @@
     far = lax.rem(y + 2, 4)
     other = 1 - core
     slots = lat_vm.shape[0]
-    sends, gots = (send0, send1), (got0, got1)
-    parts = len(LANE_TILES)
+    z, x = me // X, lax.rem(me, X)
 
     def fetch(k, source, target):
         copy = pltpu.make_async_copy(source, target, in_sem.at[k])
@@ -212,6 +207,120 @@
 
         lax.fori_loop(1, insts, ship, 0)
 
+    def wait_all(buffer, sem):
+        whole = buffer.at[pl.ds(0, buffer.shape[0] - 1)]
+        pltpu.make_async_copy(whole, whole, sem).wait()
+
+    def ship_part(source, target, k, peer):
+        pltpu.make_async_remote_copy(
+            src_ref=source,
+            dst_ref=target,
+            send_sem=att_sem.at[k, 0],
+            recv_sem=att_sem.at[k, 1],
+            device_id={"inst": peer},
+            device_id_type=MESH,
+        ).start()
+
+    def merge(got):
+        partial, stat = got[:, 0], got[:, 1]
+        peaks, totals = stat[:, :, :1], stat[:, :, TILE // 2 : TILE // 2 + 1]
+        top = jnp.max(peaks, axis=0, keepdims=True)
+        weight = jnp.exp(peaks - top)
+        return top[0], jnp.sum(partial * weight, axis=0), jnp.sum(totals * weight, axis=0)
+
+    def region(unit, h, which):
+        n = slots if unit < parts else slots // 2
+        span = {
+            None: pl.ds(0, n),
+            0: pl.ds(0, n // 2),
+            1: pl.ds(n // 2, n // 2),
+        }[which]
+        if unit < parts:
+            tiles = LANE_TILES[unit]
+            return out_lat.at[
+                span,
+                pl.ds(pl.multiple_of(h * ROWS, ROWS), ROWS),
+                pl.ds(tiles[0] * TILE, len(tiles) * TILE),
+            ]
+        return out_rope.at[h, span]
+
+    started = []
+
+    def send(unit, k, source, h, which, mate):
+        copy = pltpu.make_async_remote_copy(
+            src_ref=source,
+            dst_ref=region(unit, h, which),
+            send_sem=ag_send.at[unit, k],
+            recv_sem=ag_recv.at[unit, k],
+            device_id={"head": mate},
+            device_id_type=MESH,
+        )
+        copy.start()
+        started.append(copy)
+
+    def arrived(unit, k, h, which):
+        here = region(unit, h, which)
+        pltpu.make_async_copy(here, here, ag_recv.at[unit, k]).wait()
+
+    side, above, below = mates
+    h_up, h_down, h_far = up * 2 + core, down * 2 + core, far * 2 + core
+    o_up, o_down, o_far = up * 2 + other, down * 2 + other, far * 2 + other
+    extra = {part: [part] + [parts] * (part == ROPE_CHUNK) for part in range(parts)}
+
+    def place(part):
+        tiles = LANE_TILES[part]
+        count = len(tiles)
+        buffer = gots[part]
+        wait_all(buffer, a2a_recv.at[part])
+
+        def put(t, carry):
+            where = table_sm[t, 2]
+            g = lax.rem(me, per_row) * slots + t
+            keep = (owner_sm[me // per_row, g] >= 0) & (table_sm[t, 3] < 0)
+            spot = jnp.maximum(where, 0)
+            source, seat = spot // 2, lax.rem(spot, 2)
+            for n, tile in enumerate(tiles):
+                span = slice(tile * TILE, (tile + 1) * TILE)
+                moved = buffer[source, seat * count + n]
+                kept = share[t, :, span]
+                zero = jnp.zeros_like(moved)
+                out_lat[t, rows, span] = jnp.where(
+                    keep, kept, jnp.where(where >= 0, moved, zero)
+                )
+            if part == ROPE_CHUNK:
+                pieces = buffer[source, 2 * count].astype(jnp.float32)
+                moved = jnp.where(seat == 0, pieces[:8], pieces[8:])
+                zero = jnp.zeros_like(moved)
+                rope_got[t] = jnp.where(
+                    keep, rope_share[t], jnp.where(where >= 0, moved, zero)
+                )
+            return carry
+
+        lax.fori_loop(0, slots, put, 0, unroll=4)
+        if part == ROPE_CHUNK:
+            out_rope[head] = rope_got[...].reshape(slots // 2, ROWS, TILE).astype(jnp.bfloat16)
+        for unit in extra[part]:
+            source = region(unit, head, None)
+            send(unit, 1, source, head, None, above)
+            send(unit, 2, source, head, None, below)
+            send(unit, 0, source, head, None, side)
+
+    def relay(part):
+        for unit in extra[part]:
+            arrived(unit, 1, h_down, None)
+            send(unit, 5, region(unit, h_down, 0), h_down, 0, above)
+            send(unit, 3, region(unit, h_down, None), h_down, None, side)
+            arrived(unit, 2, h_up, None)
+            send(unit, 6, region(unit, h_up, 1), h_up, 1, below)
+            send(unit, 4, region(unit, h_up, None), h_up, None, side)
+
+    def finish(part):
+        for unit in extra[part]:
+            arrived(unit, 5, h_far, 0)
+            send(unit, 7, region(unit, h_far, 0), h_far, 0, side)
+            arrived(unit, 6, h_far, 1)
+            send(unit, 8, region(unit, h_far, 1), h_far, 1, side)
+
     heads = 16
     queries = nope_vm.shape[0]
     row_head = lax.rem(lax.broadcasted_iota(jnp.int32, (queries, 1), 0), heads)
@@ -257,6 +366,7 @@
     )
     peak = jnp.max(peak, axis=1, keepdims=True)
 
+    place(0)
     def weigh(i, carry):
         total, summed = carry
         weights = jnp.exp(scores[i] - peak)
@@ -291,182 +401,83 @@
         jnp.broadcast_to(peak, (queries, TILE)),
         jnp.broadcast_to(total, (queries, TILE)),
     )
-    att_send[:, 0] = projected.reshape(insts, 8, TILE)
-    att_send[:, 1] = stats.reshape(insts, 8, TILE)
-    att_got[me] = att_send[me]
-
-    def ship_partial(k, carry):
-        peer = lax.rem(me + k, insts)
-        pltpu.make_async_remote_copy(
-            src_ref=att_send.at[peer],
-            dst_ref=att_got.at[me],
-            send_sem=att_sem.at[0],
-            recv_sem=att_sem.at[1],
-            device_id={"inst": peer},
-            device_id_type=MESH,
-        ).start()
-        return carry
-
-    lax.fori_loop(1, insts, ship_partial, 0)
-
-    def wait_all(buffer, sem):
-        whole = buffer.at[pl.ds(0, insts - 1)]
-        pltpu.make_async_copy(whole, whole, sem).wait()
-
-    def region(unit, h, which):
-        n = slots if unit < parts else slots // 2
-        span = {
-            None: pl.ds(0, n),
-            0: pl.ds(0, n // 2),
-            1: pl.ds(n // 2, n // 2),
-        }[which]
-        if unit < parts:
-            tiles = LANE_TILES[unit]
-            return out_lat.at[
-                span,
-                pl.ds(pl.multiple_of(h * ROWS, ROWS), ROWS),
-                pl.ds(tiles[0] * TILE, len(tiles) * TILE),
-            ]
-        return out_rope.at[h, span]
-
-    def own_region(unit):
-        if unit < parts:
-            tiles = LANE_TILES[unit]
-            return landed.at[:, :, pl.ds(tiles[0] * TILE, len(tiles) * TILE)]
-        return landed_rope
-
-    started = []
-
-    def send(unit, k, source, h, which, mate):
-        copy = pltpu.make_async_remote_copy(
-            src_ref=source,
-            dst_ref=region(unit, h, which),
-            send_sem=ag_send.at[unit, k],
-            recv_sem=ag_recv.at[unit, k],
-            device_id={"head": mate},
-            device_id_type=MESH,
-        )
-        copy.start()
-        started.append(copy)
-
-    def arrived(unit, k, h, which):
-        here = region(unit, h, which)
-        pltpu.make_async_copy(here, here, ag_recv.at[unit, k]).wait()
-
-    side, above, below = mates
-    h_up, h_down, h_far = up * 2 + core, down * 2 + core, far * 2 + core
-    o_up, o_down, o_far = up * 2 + other, down * 2 + other, far * 2 + other
-    keeping = []
-
-    def place_part(part):
-        tiles = LANE_TILES[part]
-        count = len(tiles)
-        buffer = gots[part]
-        wait_all(buffer, a2a_recv.at[part])
-
-        def put(t, carry):
-            where = table_sm[t, 2]
-            g = lax.rem(me, per_row) * slots + t
-            keep = (owner_sm[me // per_row, g] >= 0) & (table_sm[t, 3] < 0)
-            spot = jnp.maximum(where, 0)
-            source, seat = spot // 2, lax.rem(spot, 2)
-            for n, tile in enumerate(tiles):
-                span = slice(tile * TILE, (tile + 1) * TILE)
-                moved = buffer[source, seat * count + n]
-                kept = share[t, :, span]
-                zero = jnp.zeros_like(moved)
-                landed[t, :, span] = jnp.where(
-                    keep, kept, jnp.where(where >= 0, moved, zero)
-                )
-            if part == ROPE_CHUNK:
-                pieces = buffer[source, 2 * count].astype(jnp.float32)
-                moved = jnp.where(seat == 0, pieces[:8], pieces[8:])
-                zero = jnp.zeros_like(moved)
-                rope_got[t] = jnp.where(
-                    keep, rope_share[t], jnp.where(where >= 0, moved, zero)
-                )
-            return carry
-
-        lax.fori_loop(0, slots, put, 0, unroll=4)
-        units = [part]
-        if part == ROPE_CHUNK:
-            landed_rope[...] = (
-                rope_got[...].reshape(slots // 2, ROWS, TILE).astype(jnp.bfloat16)
-            )
-            units.append(parts)
-        for unit in units:
-            source = own_region(unit)
-            copy = pltpu.make_async_copy(source, region(unit, head, None), own_sem.at[unit])
-            copy.start()
-            keeping.append(copy)
-            send(unit, 1, source, head, None, above)
-            send(unit, 2, source, head, None, below)
-            send(unit, 0, source, head, None, side)
-
-    def relay(unit):
-        arrived(unit, 1, h_down, None)
-        send(unit, 5, region(unit, h_down, 0), h_down, 0, above)
-        send(unit, 3, region(unit, h_down, None), h_down, None, side)
-        arrived(unit, 2, h_up, None)
-        send(unit, 6, region(unit, h_up, 1), h_up, 1, below)
-        send(unit, 4, region(unit, h_up, None), h_up, None, side)
-
-    def finish(unit):
-        arrived(unit, 5, h_far, 0)
-        send(unit, 7, region(unit, h_far, 0), h_far, 0, side)
-        arrived(unit, 6, h_far, 1)
-        send(unit, 8, region(unit, h_far, 1), h_far, 1, side)
-
-    def combine():
-        wait_all(att_got, att_sem.at[1])
-        got = att_got[...]
-        partial, stat = got[:, 0], got[:, 1]
-        peaks, totals = stat[:, :, :1], stat[:, :, TILE // 2 : TILE // 2 + 1]
-        top = jnp.max(peaks, axis=0, keepdims=True)
-        weight = jnp.exp(peaks - top)
-        above_line = jnp.sum(partial * weight, axis=0)
-        below_line = jnp.sum(totals * weight, axis=0)
-        att_all[me] = above_line / below_line
-
-        def ship_result(k, carry):
-            pltpu.make_async_remote_copy(
-                src_ref=att_all.at[me],
-                dst_ref=att_all.at[me],
-                send_sem=att_sem.at[2],
-                recv_sem=att_sem.at[3],
-                device_id={"inst": lax.rem(me + k, insts)},
-                device_id_type=MESH,
-            ).start()
-            return carry
-
-        lax.fori_loop(1, insts, ship_result, 0)
-
-    place_part(0)
-    combine()
-    place_part(1)
+    x_send[:, 0] = projected.reshape(X, queries // X, TILE)
+    x_send[:, 1] = stats.reshape(X, queries // X, TILE)
+    x_got[x] = x_send[x]
+    for k in range(1, X):
+        peer = lax.rem(x + k, X)
+        ship_part(x_send.at[peer], x_got.at[x], 0, z * X + peer)
+    place(1)
     relay(0)
+
+    wait_all(x_got, att_sem.at[0, 1])
+    top, sums, totals = merge(x_got[...])
+    z_send[:, 0] = sums.reshape(Z, 8, TILE)
+    z_send[:, 1] = jnp.where(wide[: queries // X] < TILE // 2, top, totals).reshape(Z, 8, TILE)
+    z_got[z] = z_send[z]
+    for k in range(1, Z):
+        peer = lax.rem(z + k, Z)
+        ship_part(z_send.at[peer], z_got.at[z], 1, peer * X + x)
+    place(2)
     relay(1)
+    finish(0)
+
+    wait_all(z_got, att_sem.at[1, 1])
+    top, sums, totals = merge(z_got[...])
+    z_all[z] = sums / totals
+    for k in range(1, Z):
+        ship_part(z_all.at[z], z_all.at[z], 2, lax.rem(z + k, Z) * X + x)
+    place(3)
     relay(2)
-    finish(0)
     finish(1)
+    wait_all(z_all, att_sem.at[2, 1])
+    x_all[x] = z_all[...].reshape(queries // X, TILE)
+    for k in range(1, X):
+        ship_part(x_all.at[x], x_all.at[x], 3, z * X + lax.rem(x + k, X))
+    relay(3)
     finish(2)
-
-    wait_all(att_all, att_sem.at[3])
-    out_att[...] = att_all[...].reshape(queries, TILE)
+    wait_all(x_all, att_sem.at[3, 1])
+    out_att[...] = x_all[...].reshape(queries, TILE)
+    finish(3)
+
     for unit in range(parts + 1):
         arrived(unit, 0, y * 2 + other, None)
         arrived(unit, 3, o_down, None)
         arrived(unit, 4, o_up, None)
         arrived(unit, 7, o_far, 0)
         arrived(unit, 8, o_far, 1)
-    for copy in keeping:
-        copy.wait()
     for copy in started:
         copy.wait_send()
     for part in range(parts):
         wait_all(sends[part], a2a_send.at[part])
-    wait_all(att_send, att_sem.at[0])
-    wait_all(att_all, att_sem.at[2])
+    wait_all(x_send, att_sem.at[0, 0])
+    wait_all(z_send, att_sem.at[1, 0])
+    wait_all(z_all, att_sem.at[2, 0])
+    wait_all(x_all, att_sem.at[3, 0])
+
+
+def hand_out(att, lat, rope, out_att, out_lat, out_rope, turned, sem):
+    first = pltpu.make_async_copy(lat, out_lat, sem.at[0])
+    first.start()
+    second = pltpu.make_async_copy(att, out_att, sem.at[1])
+    second.start()
+
+    def turn(p, carry):
+        for n in range(rope.shape[0] // 2):
+            low = rope[2 * n, p].astype(jnp.float32)
+            high = rope[2 * n + 1, p].astype(jnp.float32)
+            for b in range(2):
+                span = slice(8 * b, 8 * b + 8)
+                both = jnp.concatenate([low[span], high[span]], axis=0)
+                turned[2 * p + b, ROWS * n : ROWS * (n + 1), :] = both.astype(jnp.bfloat16)
+        return carry
+
+    lax.fori_loop(0, rope.shape[1], turn, 0, unroll=2)
+    third = pltpu.make_async_copy(turned, out_rope, sem.at[2])
+    third.start()
+    first.wait()
+    second.wait()
+    third.wait()
 
 
 def shards(
@@ -496,12 +507,12 @@
     attention, moved, rope = pl.pallas_call(
         kernel,
         out_shape=(
-            jax.ShapeDtypeStruct((queries, TILE), f32),
-            jax.ShapeDtypeStruct(latent_cache.shape, bf16),
-            jax.ShapeDtypeStruct((heads_axis, slots // 2, ROWS, TILE), bf16),
+            pltpu.VMEM((queries, TILE), f32),
+            pltpu.VMEM(latent_cache.shape, bf16),
+            pltpu.VMEM((heads_axis, slots // 2, ROWS, TILE), bf16),
         ),
-        in_specs=[anywhere] * 10,
-        out_specs=(pl.BlockSpec(memory_space=pltpu.VMEM), anywhere, anywhere),
+        in_specs=[pl.BlockSpec(memory_space=pltpu.HBM)] * 10,
+        out_specs=(pl.BlockSpec(memory_space=pltpu.VMEM),) * 3,
         scratch_shapes=[
             pltpu.VMEM((slots, block, width), bf16),
             pltpu.VMEM((slots, rope_width, block), bf16),
@@ -517,14 +528,15 @@
             pltpu.SMEM((slots, TILE), i32),
             pltpu.VMEM((slots, ROWS, width), bf16),
             pltpu.VMEM((slots, 8, TILE), f32),
-            pltpu.VMEM((slots, ROWS, width), bf16),
-            pltpu.VMEM((slots // 2, ROWS, TILE), bf16),
             pltpu.VMEM((slots, 8, TILE), f32),
             pltpu.VMEM((queries, width), bf16),
             pltpu.VMEM((slots // 2, queries, 2 * TILE), f32),
-            pltpu.VMEM((insts, 2, 8, TILE), f32),
-            pltpu.VMEM((insts, 2, 8, TILE), f32),
-            pltpu.VMEM((insts, 8, TILE), f32),
+            pltpu.VMEM((X, 2, queries // X, TILE), f32),
+            pltpu.VMEM((X, 2, queries // X, TILE), f32),
+            pltpu.VMEM((Z, 2, 8, TILE), f32),
+            pltpu.VMEM((Z, 2, 8, TILE), f32),
+            pltpu.VMEM((Z, 8, TILE), f32),
+            pltpu.VMEM((X, queries // X, TILE), f32),
         ]
         + [pltpu.VMEM((insts, n, ROWS, TILE), bf16) for n in tiles]
         + [pltpu.VMEM((insts, n, ROWS, TILE), bf16) for n in tiles]
@@ -532,30 +544,50 @@
             pltpu.SemaphoreType.DMA((12,)),
             pltpu.SemaphoreType.DMA((len(tiles),)),
             pltpu.SemaphoreType.DMA((len(tiles),)),
-            pltpu.SemaphoreType.DMA((4,)),
-            pltpu.SemaphoreType.DMA((units,)),
+            pltpu.SemaphoreType.DMA((4, 2)),
             pltpu.SemaphoreType.DMA((units, 9)),
             pltpu.SemaphoreType.DMA((units, 9)),
         ],
         compiler_params=pltpu.CompilerParams(
-            collective_id=0, has_side_effects=True, vmem_limit_bytes=56 * 2**20
+            collective_id=0, has_side_effects=True, vmem_limit_bytes=40 * 2**20
         ),
         name="decode_and_move",
     )(
-        latent_cache,
-        rope_cache.swapaxes(1, 2),
-        query_nope.reshape(queries, nope_width),
-        query_rope.reshape(queries, rope_width),
-        key_absorb,
-        value_up_weight,
-        block_request.reshape(8, TILE),
-        block_index.reshape(8, TILE),
-        request_length,
-        move_plan.reshape(8, TILE),
-    )
-    rope = rope.reshape(heads_axis, slots, 8, TILE).swapaxes(0, 1)
-    rope = rope.reshape(slots, rope_width, block).swapaxes(1, 2)
-    return attention.reshape(steps, requests, heads, TILE), moved, rope
+        *(
+            pltpu.with_memory_space_constraint(a, pltpu.HBM)
+            for a in (
+                latent_cache,
+                rope_cache.swapaxes(1, 2),
+                query_nope.reshape(queries, nope_width),
+                query_rope.reshape(queries, rope_width),
+                key_absorb,
+                value_up_weight,
+                block_request.reshape(8, TILE),
+                block_index.reshape(8, TILE),
+                request_length,
+                move_plan.reshape(8, TILE),
+            )
+        )
+    )
+    inside = [pltpu.with_memory_space_constraint(a, pltpu.VMEM) for a in (attention, moved, rope)]
+    attention, moved, rope = pl.pallas_call(
+        hand_out,
+        out_shape=(
+            jax.ShapeDtypeStruct((queries, TILE), f32),
+            jax.ShapeDtypeStruct(latent_cache.shape, bf16),
+            jax.ShapeDtypeStruct((slots, rope_width, block), bf16),
+        ),
+        in_specs=[pl.BlockSpec(memory_space=pltpu.VMEM)] * 3,
+        out_specs=(anywhere,) * 3,
+        scratch_shapes=[
+            pltpu.VMEM((slots, rope_width, block), bf16),
+            pltpu.SemaphoreType.DMA((3,)),
+        ],
+        compiler_params=pltpu.CompilerParams(vmem_limit_bytes=16 * 2**20),
+        name="hand_out",
+    )(*inside)
+    attention = attention.reshape(steps, requests, heads, TILE)
+    return attention, moved, rope.swapaxes(1, 2)
 
 
 def solution(mesh):

time: 72.7 us -> 58.6 us (0.81)
  local copies, waits for them, and re-layouts: 8.18 us -> 0 us
  Pallas kernels: 63.7 us -> 57.8 us
    unnamed x2 -> x0, local copies, waits for them, and re-layouts: 6.2 us -> none
    pallas_call x1 -> x2, Pallas kernels: 63.7 us -> 57.8 us  [the longest x1 55.6 us: shards(): pl.pallas_call(kernel, out_shape=(pltpu.VMEM((queries, TILE), f32), pltpu...]
    transpose x1 -> x0, local copies, waits for them, and re-layouts: 1.98 us -> none  [shards(): rope = rope.reshape(heads_axis, slots, 8, TILE).swapaxes(0, 1)]
where the time goes in v2:
time: 58.6 us; the launch traced here: 58.5 us
  Pallas kernels  57.8 us (99%)
  between operations  0.64 us (1%)
    pallas_call x1, Pallas kernels, shards(): pl.pallas_call(kernel, out_shape=(pltpu.VMEM((queries, TILE), f32), pltpu...  55.6 us
    pallas_call x1, Pallas kernels, shards(): pl.pallas_call(hand_out, out_shape=(jax.ShapeDtypeStruct((queries, TILE),...  2.24 us

profile of v2, /device:TPU:1, one launch (start us, length us, event | category | flops | bytes accessed | tf_op | source)
XLA Modules:
  0.0 58.5 jit_solution(6822286617696484055)
XLA Ops:
  0.6 55.6 %decode_and_move.1 = (f32[256,128]{1,0:T(8,128)S(1)}, bf16[32,128,512]{2,1,0:T(8,128)(2,1)S(1)}, bf16[8,16,16,128]{3,2,1,0:T(8,128)(2,1)S(1)}) custom-call(bf16[32,128,512]{2,1,0:T(8,128)(2,1)} %lat_hbm.1, bf16[32,64,128]{2,1,0:T(8,128)(2,1)} %bitcast.8, bf16[256,128]{1,0:T(8,128)(2,1)} %bitcast.9, bf16[256,64]{1,0:T(8,128)(2,1)} %bitcast.10, ...), custom_call_target="tpu_custom_call" | custom-call | tf_op jit(solution)/shard_map/decode_and_move/pallas_call | solution.py:507
  56.2 2.2 %hand_out.1 = (f32[256,128]{1,0:T(8,128)}, bf16[32,128,512]{2,1,0:T(8,128)(2,1)}, bf16[32,64,128]{2,1,0:T(8,128)(2,1)}) custom-call(f32[256,128]{1,0:T(8,128)S(1)} %get-tuple-element.9.att, bf16[32,128,512]{2,1,0:T(8,128)(2,1)S(1)} %get-tuple-element.10.lat, bf16[8,16,16,128]{3,2,1,0:T(8,128)(2,1)S(1)} %get-tuple-element.11.rope), custom_call_target="tpu_custom_call" | custom-call | tf_op jit(solution)/shard_map/hand_out/pallas_call | solution.py:573

commit v3 on v2

--- a/solution.py
+++ b/solution.py
@@ -12,10 +12,14 @@
 FLOOR = -1e29
 TILE = 128
 ROWS = 16
-LANE_TILES = ((0,), (1,), (2,), (3,))
+LANE_TILES = ((0,),(1,),(2,),(3,))
 ROPE_CHUNK = 0
+WINDOW = 9
+PIECES = 8
 Z, X = 8, 4
 NEG = -1
+ABSORB = 8
+UNROLL = 4
 
 
 def kernel(
@@ -103,7 +107,7 @@
         return carry
 
     lax.fori_loop(1, insts, greet, 0)
-    mates = (y * 2 + other, up * 2 + core, down * 2 + core)
+    mates = (y * 2 + other, up * 2 + core, down * 2 + core, far * 2 + core)
     for mate in mates:
         pl.semaphore_signal(barrier, inc=1, device_id={"head": mate}, device_id_type=MESH)
 
@@ -171,12 +175,14 @@
     get_index.wait()
     get_length.wait()
 
-    for part in range(parts):
+    def dispatch(part):
+        if part >= parts:
+            return
         tiles = LANE_TILES[part]
         count = len(tiles)
         buffer = sends[part]
 
-        def pack(j, carry, tiles=tiles, count=count, buffer=buffer, part=part):
+        def pack(j, carry):
             picks = (table_sm[j, 0], table_sm[j, 1])
             for seat in range(2):
                 for n, tile in enumerate(tiles):
@@ -193,7 +199,7 @@
         if part == 0:
             pl.semaphore_wait(barrier, insts - 1 + len(mates))
 
-        def ship(k, carry, part=part, buffer=buffer):
+        def ship(k, carry):
             peer = lax.rem(me + k, insts)
             pltpu.make_async_remote_copy(
                 src_ref=buffer.at[peer],
@@ -206,6 +212,9 @@
             return carry
 
         lax.fori_loop(1, insts, ship, 0)
+
+    for part in range(min(WINDOW, parts)):
+        dispatch(part)
 
     def wait_all(buffer, sem):
         whole = buffer.at[pl.ds(0, buffer.shape[0] - 1)]
@@ -262,16 +271,18 @@
         here = region(unit, h, which)
         pltpu.make_async_copy(here, here, ag_recv.at[unit, k]).wait()
 
-    side, above, below = mates
+    side, above, below, _ = mates
     h_up, h_down, h_far = up * 2 + core, down * 2 + core, far * 2 + core
     o_up, o_down, o_far = up * 2 + other, down * 2 + other, far * 2 + other
-    extra = {part: [part] + [parts] * (part == ROPE_CHUNK) for part in range(parts)}
+    extra = {p: [p] * (len(LANE_TILES[p]) > 0) + [parts] * (p == ROPE_CHUNK) for p in range(parts)}
+    units = [unit for p in range(parts) for unit in extra[p]]
 
     def place(part):
         tiles = LANE_TILES[part]
         count = len(tiles)
         buffer = gots[part]
         wait_all(buffer, a2a_recv.at[part])
+        dispatch(part + WINDOW)
 
         def put(t, carry):
             where = table_sm[t, 2]
@@ -303,9 +314,18 @@
             source = region(unit, head, None)
             send(unit, 1, source, head, None, above)
             send(unit, 2, source, head, None, below)
+            if part == parts - 1:
+                send(unit, 5, source, head, None, far * 2 + core)
             send(unit, 0, source, head, None, side)
 
     def relay(part):
+        if part == parts - 1:
+            for unit in extra[part]:
+                arrived(unit, 1, h_down, None)
+                send(unit, 3, region(unit, h_down, None), h_down, None, side)
+                arrived(unit, 2, h_up, None)
+                send(unit, 4, region(unit, h_up, None), h_up, None, side)
+            return
         for unit in extra[part]:
             arrived(unit, 1, h_down, None)
             send(unit, 5, region(unit, h_down, 0), h_down, 0, above)
@@ -315,6 +335,11 @@
             send(unit, 4, region(unit, h_up, None), h_up, None, side)
 
     def finish(part):
+        if part == parts - 1:
+            for unit in extra[part]:
+                arrived(unit, 5, h_far, None)
+                send(unit, 7, region(unit, h_far, None), h_far, None, side)
+            return
         for unit in extra[part]:
             arrived(unit, 5, h_far, 0)
             send(unit, 7, region(unit, h_far, 0), h_far, 0, side)
@@ -329,11 +354,19 @@
     get_absorb.wait()
     width = lat_vm.shape[2]
 
-    def absorb(h, total):
-        part_query = jnp.where(row_head == h, nope_vm[...], jnp.zeros((), jnp.bfloat16))
-        return total + jnp.dot(part_query, absorb_vm[h], preferred_element_type=jnp.float32)
-
-    absorbed = lax.fori_loop(0, heads, absorb, jnp.zeros((queries, width), jnp.float32))
+    def absorb(n, total):
+        part_query = [
+            jnp.where(row_head == ABSORB * n + h, nope_vm[...], jnp.zeros((), jnp.bfloat16))
+            for h in range(ABSORB)
+        ]
+        weights = absorb_vm[pl.ds(ABSORB * n, ABSORB)].reshape(ABSORB * TILE, width)
+        return total + jnp.dot(
+            jnp.concatenate(part_query, axis=1), weights, preferred_element_type=jnp.float32
+        )
+
+    absorbed = lax.fori_loop(
+        0, heads // ABSORB, absorb, jnp.zeros((queries, width), jnp.float32)
+    )
     query[...] = absorbed.astype(jnp.bfloat16)
     get_qrope.wait()
     get_lat.wait()
@@ -362,11 +395,10 @@
         return jnp.maximum(peak, raw)
 
     peak = lax.fori_loop(
-        0, slots // 2, score, jnp.full((queries, pair), FLOOR, jnp.float32)
+        0, slots // 2, score, jnp.full((queries, pair), FLOOR, jnp.float32), unroll=UNROLL
     )
     peak = jnp.max(peak, axis=1, keepdims=True)
 
-    place(0)
     def weigh(i, carry):
         total, summed = carry
         weights = jnp.exp(scores[i] - peak)
@@ -381,6 +413,7 @@
         slots // 2,
         weigh,
         (jnp.zeros((queries, pair), jnp.float32), jnp.zeros((queries, width), jnp.float32)),
+        unroll=UNROLL,
     )
     total = jnp.sum(total, axis=1, keepdims=True)
     query[...] = summed.astype(jnp.bfloat16)
@@ -393,7 +426,7 @@
         return jnp.where(row_head == 2 * n + 1, got[:, TILE:], result)
 
     projected = lax.fori_loop(
-        0, heads // 2, project, jnp.zeros((queries, TILE), jnp.float32)
+        0, heads // 2, project, jnp.zeros((queries, TILE), jnp.float32), unroll=UNROLL
     )
     wide = lax.broadcasted_iota(jnp.int32, (queries, TILE), 1)
     stats = jnp.where(
@@ -407,6 +440,7 @@
     for k in range(1, X):
         peer = lax.rem(x + k, X)
         ship_part(x_send.at[peer], x_got.at[x], 0, z * X + peer)
+    place(0)
     place(1)
     relay(0)
 
@@ -418,34 +452,45 @@
     for k in range(1, Z):
         peer = lax.rem(z + k, Z)
         ship_part(z_send.at[peer], z_got.at[z], 1, peer * X + x)
-    place(2)
-    relay(1)
-    finish(0)
-
-    wait_all(z_got, att_sem.at[1, 1])
-    top, sums, totals = merge(z_got[...])
-    z_all[z] = sums / totals
-    for k in range(1, Z):
-        ship_part(z_all.at[z], z_all.at[z], 2, lax.rem(z + k, Z) * X + x)
-    place(3)
-    relay(2)
-    finish(1)
-    wait_all(z_all, att_sem.at[2, 1])
-    x_all[x] = z_all[...].reshape(queries // X, TILE)
-    for k in range(1, X):
-        ship_part(x_all.at[x], x_all.at[x], 3, z * X + lax.rem(x + k, X))
-    relay(3)
-    finish(2)
+
+    def second():
+        wait_all(z_got, att_sem.at[1, 1])
+        top, sums, totals = merge(z_got[...])
+        z_all[z] = sums / totals
+        for k in range(1, Z):
+            ship_part(z_all.at[z], z_all.at[z], 2, lax.rem(z + k, Z) * X + x)
+
+    def third():
+        wait_all(z_all, att_sem.at[2, 1])
+        x_all[x] = z_all[...].reshape(queries // X, TILE)
+        for k in range(1, X):
+            ship_part(x_all.at[x], x_all.at[x], 3, z * X + lax.rem(x + k, X))
+
+    for part in range(2, parts):
+        relay(part - 1)
+        place(part)
+        finish(part - 2)
+        if part == 2:
+            second()
+        if part == 3:
+            third()
+    relay(parts - 1)
+    finish(parts - 2)
+    if parts <= 3:
+        third()
+    finish(parts - 1)
     wait_all(x_all, att_sem.at[3, 1])
     out_att[...] = x_all[...].reshape(queries, TILE)
-    finish(3)
-
-    for unit in range(parts + 1):
+
+    for unit in units:
         arrived(unit, 0, y * 2 + other, None)
         arrived(unit, 3, o_down, None)
         arrived(unit, 4, o_up, None)
-        arrived(unit, 7, o_far, 0)
-        arrived(unit, 8, o_far, 1)
+        if unit in extra[parts - 1]:
+            arrived(unit, 7, o_far, None)
+        else:
+            arrived(unit, 7, o_far, 0)
+            arrived(unit, 8, o_far, 1)
     for copy in started:
         copy.wait_send()
     for part in range(parts):
@@ -457,8 +502,12 @@
 
 
 def hand_out(att, lat, rope, out_att, out_lat, out_rope, turned, sem):
-    first = pltpu.make_async_copy(lat, out_lat, sem.at[0])
-    first.start()
+    step = lat.shape[0] // PIECES
+    copies = []
+    for n in range(PIECES):
+        span = pl.ds(n * step, step)
+        copies.append(pltpu.make_async_copy(lat.at[span], out_lat.at[span], sem.at[3 + n]))
+        copies[-1].start()
     second = pltpu.make_async_copy(att, out_att, sem.at[1])
     second.start()
 
@@ -475,7 +524,8 @@
     lax.fori_loop(0, rope.shape[1], turn, 0, unroll=2)
     third = pltpu.make_async_copy(turned, out_rope, sem.at[2])
     third.start()
-    first.wait()
+    for copy in copies:
+        copy.wait()
     second.wait()
     third.wait()
 
@@ -581,7 +631,7 @@
         out_specs=(anywhere,) * 3,
         scratch_shapes=[
             pltpu.VMEM((slots, rope_width, block), bf16),
-            pltpu.SemaphoreType.DMA((3,)),
+            pltpu.SemaphoreType.DMA((3 + PIECES,)),
         ],
         compiler_params=pltpu.CompilerParams(vmem_limit_bytes=16 * 2**20),
         name="hand_out",

time: 58.6 us -> 55.3 us (0.944)
  Pallas kernels: 57.8 us -> 54.6 us
    pallas_call x1, Pallas kernels: 55.6 us -> 52.3 us  [shards(): pl.pallas_call(kernel, out_shape=(pltpu.VMEM((queries, TILE), f32), pltpu...]
where the time goes in v3:
time: 55.3 us; the launch traced here: 55.2 us
  Pallas kernels  54.6 us (99%)
  between operations  0.64 us (1%)
    pallas_call x1, Pallas kernels, shards(): pl.pallas_call(kernel, out_shape=(pltpu.VMEM((queries, TILE), f32), pltpu...  52.3 us
    pallas_call x1, Pallas kernels, shards(): pl.pallas_call(hand_out, out_shape=(jax.ShapeDtypeStruct((queries, TILE),...  2.31 us

profile of v3, /device:TPU:1, one launch (start us, length us, event | category | flops | bytes accessed | tf_op | source)
XLA Modules:
  0.0 55.2 jit_solution(2614891150067906863)
XLA Ops:
  0.6 52.3 %decode_and_move.1 = (f32[256,128]{1,0:T(8,128)S(1)}, bf16[32,128,512]{2,1,0:T(8,128)(2,1)S(1)}, bf16[8,16,16,128]{3,2,1,0:T(8,128)(2,1)S(1)}) custom-call(bf16[32,128,512]{2,1,0:T(8,128)(2,1)} %lat_hbm.1, bf16[32,64,128]{2,1,0:T(8,128)(2,1)} %bitcast.8, bf16[256,128]{1,0:T(8,128)(2,1)} %bitcast.9, bf16[256,64]{1,0:T(8,128)(2,1)} %bitcast.10, ...), custom_call_target="tpu_custom_call" | custom-call | tf_op jit(solution)/shard_map/decode_and_move/pallas_call | solution.py:557
  52.9 2.3 %hand_out.1 = (f32[256,128]{1,0:T(8,128)}, bf16[32,128,512]{2,1,0:T(8,128)(2,1)}, bf16[32,64,128]{2,1,0:T(8,128)(2,1)}) custom-call(f32[256,128]{1,0:T(8,128)S(1)} %get-tuple-element.9.att, bf16[32,128,512]{2,1,0:T(8,128)(2,1)S(1)} %get-tuple-element.10.lat, bf16[8,16,16,128]{3,2,1,0:T(8,128)(2,1)S(1)} %get-tuple-element.11.rope), custom_call_target="tpu_custom_call" | custom-call | tf_op jit(solution)/shard_map/hand_out/pallas_call | solution.py:623

commit v4 on v3

--- a/solution.py
+++ b/solution.py
@@ -14,9 +14,10 @@
 ROWS = 16
 LANE_TILES = ((0,),(1,),(2,),(3,))
 ROPE_CHUNK = 0
-WINDOW = 9
+WINDOW = 2
 PIECES = 8
 Z, X = 8, 4
+ROW_ORDER = (0, 1, 2, 3, 7, 4, 5, 6)
 NEG = -1
 ABSORB = 8
 UNROLL = 4
@@ -200,18 +201,23 @@
             pl.semaphore_wait(barrier, insts - 1 + len(mates))
 
         def ship(k, carry):
-            peer = lax.rem(me + k, insts)
-            pltpu.make_async_remote_copy(
-                src_ref=buffer.at[peer],
-                dst_ref=gots[part].at[me],
-                send_sem=a2a_send.at[part],
-                recv_sem=a2a_recv.at[part],
-                device_id={"inst": peer},
-                device_id_type=MESH,
-            ).start()
+            peer = carry * X + lax.rem(x + k, X)
+
+            @pl.when(peer != me)
+            def _():
+                pltpu.make_async_remote_copy(
+                    src_ref=buffer.at[peer],
+                    dst_ref=gots[part].at[me],
+                    send_sem=a2a_send.at[part],
+                    recv_sem=a2a_recv.at[part],
+                    device_id={"inst": peer},
+                    device_id_type=MESH,
+                ).start()
+
             return carry
 
-        lax.fori_loop(1, insts, ship, 0)
+        for row in ROW_ORDER:
+            lax.fori_loop(0, X, ship, row)
 
     for part in range(min(WINDOW, parts)):
         dispatch(part)
@@ -440,18 +446,15 @@
     for k in range(1, X):
         peer = lax.rem(x + k, X)
         ship_part(x_send.at[peer], x_got.at[x], 0, z * X + peer)
-    place(0)
-    place(1)
-    relay(0)
-
-    wait_all(x_got, att_sem.at[0, 1])
-    top, sums, totals = merge(x_got[...])
-    z_send[:, 0] = sums.reshape(Z, 8, TILE)
-    z_send[:, 1] = jnp.where(wide[: queries // X] < TILE // 2, top, totals).reshape(Z, 8, TILE)
-    z_got[z] = z_send[z]
-    for k in range(1, Z):
-        peer = lax.rem(z + k, Z)
-        ship_part(z_send.at[peer], z_got.at[z], 1, peer * X + x)
+    def first():
+        wait_all(x_got, att_sem.at[0, 1])
+        top, sums, totals = merge(x_got[...])
+        z_send[:, 0] = sums.reshape(Z, 8, TILE)
+        z_send[:, 1] = jnp.where(wide[: queries // X] < TILE // 2, top, totals).reshape(Z, 8, TILE)
+        z_got[z] = z_send[z]
+        for k in range(1, Z):
+            peer = lax.rem(z + k, Z)
+            ship_part(z_send.at[peer], z_got.at[z], 1, peer * X + x)
 
     def second():
         wait_all(z_got, att_sem.at[1, 1])
@@ -466,19 +469,21 @@
         for k in range(1, X):
             ship_part(x_all.at[x], x_all.at[x], 3, z * X + lax.rem(x + k, X))
 
-    for part in range(2, parts):
-        relay(part - 1)
-        place(part)
-        finish(part - 2)
-        if part == 2:
-            second()
-        if part == 3:
-            third()
-    relay(parts - 1)
-    finish(parts - 2)
-    if parts <= 3:
-        third()
-    finish(parts - 1)
+    place(0)
+    first()
+    place(1)
+    relay(0)
+    relay(1)
+    place(2)
+    finish(0)
+    second()
+    relay(2)
+    place(3)
+    finish(1)
+    finish(2)
+    third()
+    relay(3)
+    finish(3)
     wait_all(x_all, att_sem.at[3, 1])
     out_att[...] = x_all[...].reshape(queries, TILE)
 

time: 55.3 us -> 53.3 us (0.964)
  Pallas kernels: 54.6 us -> 52 us
    pallas_call x1, Pallas kernels: 52.3 us -> 49.7 us  [shards(): pl.pallas_call(kernel, out_shape=(pltpu.VMEM((queries, TILE), f32), pltpu...]
where the time goes in v4:
time: 53.3 us; the launch traced here: 52.7 us
  Pallas kernels  52 us (98%)
  between operations  0.64 us (1%)
    pallas_call x1, Pallas kernels, shards(): pl.pallas_call(kernel, out_shape=(pltpu.VMEM((queries, TILE), f32), pltpu...  49.7 us
    pallas_call x1, Pallas kernels, shards(): pl.pallas_call(hand_out, out_shape=(jax.ShapeDtypeStruct((queries, TILE),...  2.31 us

profile of v4, /device:TPU:1, one launch (start us, length us, event | category | flops | bytes accessed | tf_op | source)
XLA Modules:
  0.0 52.7 jit_solution(12112379476649020148)
XLA Ops:
  0.6 49.7 %decode_and_move.1 = (f32[256,128]{1,0:T(8,128)S(1)}, bf16[32,128,512]{2,1,0:T(8,128)(2,1)S(1)}, bf16[8,16,16,128]{3,2,1,0:T(8,128)(2,1)S(1)}) custom-call(bf16[32,128,512]{2,1,0:T(8,128)(2,1)} %lat_hbm.1, bf16[32,64,128]{2,1,0:T(8,128)(2,1)} %bitcast.8, bf16[256,128]{1,0:T(8,128)(2,1)} %bitcast.9, bf16[256,64]{1,0:T(8,128)(2,1)} %bitcast.10, ...), custom_call_target="tpu_custom_call" | custom-call | tf_op jit(solution)/shard_map/decode_and_move/pallas_call | solution.py:562
  50.4 2.3 %hand_out.1 = (f32[256,128]{1,0:T(8,128)}, bf16[32,128,512]{2,1,0:T(8,128)(2,1)}, bf16[32,64,128]{2,1,0:T(8,128)(2,1)}) custom-call(f32[256,128]{1,0:T(8,128)S(1)} %get-tuple-element.9.att, bf16[32,128,512]{2,1,0:T(8,128)(2,1)S(1)} %get-tuple-element.10.lat, bf16[8,16,16,128]{3,2,1,0:T(8,128)(2,1)S(1)} %get-tuple-element.11.rope), custom_call_target="tpu_custom_call" | custom-call | tf_op jit(solution)/shard_map/hand_out/pallas_call | solution.py:628

commit v5 on v4

--- a/solution.py
+++ b/solution.py
@@ -196,7 +196,7 @@
                 ).astype(jnp.bfloat16)
             return carry
 
-        lax.fori_loop(0, insts, pack, 0, unroll=4)
+        lax.fori_loop(0, insts, pack, 0, unroll=8)
         if part == 0:
             pl.semaphore_wait(barrier, insts - 1 + len(mates))
 
@@ -313,15 +313,15 @@
                 )
             return carry
 
-        lax.fori_loop(0, slots, put, 0, unroll=4)
+        lax.fori_loop(0, slots, put, 0, unroll=16)
         if part == ROPE_CHUNK:
             out_rope[head] = rope_got[...].reshape(slots // 2, ROWS, TILE).astype(jnp.bfloat16)
         for unit in extra[part]:
             source = region(unit, head, None)
+            if part == parts - 1:
+                send(unit, 5, source, head, None, far * 2 + core)
             send(unit, 1, source, head, None, above)
             send(unit, 2, source, head, None, below)
-            if part == parts - 1:
-                send(unit, 5, source, head, None, far * 2 + core)
             send(unit, 0, source, head, None, side)
 
     def relay(part):

time: 53.3 us -> 53.2 us (level)
  no operation moved by 1% of the time
where the time goes in v5:
time: 53.2 us; the launch traced here: 52.9 us
  Pallas kernels  52.2 us (98%)
  between operations  0.64 us (1%)
    pallas_call x1, Pallas kernels, shards(): pl.pallas_call(kernel, out_shape=(pltpu.VMEM((queries, TILE), f32), pltpu...  49.9 us
    pallas_call x1, Pallas kernels, shards(): pl.pallas_call(hand_out, out_shape=(jax.ShapeDtypeStruct((queries, TILE),...  2.31 us

profile of v5, /device:TPU:1, one launch (start us, length us, event | category | flops | bytes accessed | tf_op | source)
XLA Modules:
  0.0 52.9 jit_solution(8550923227837460366)
XLA Ops:
  0.6 49.9 %decode_and_move.1 = (f32[256,128]{1,0:T(8,128)S(1)}, bf16[32,128,512]{2,1,0:T(8,128)(2,1)S(1)}, bf16[8,16,16,128]{3,2,1,0:T(8,128)(2,1)S(1)}) custom-call(bf16[32,128,512]{2,1,0:T(8,128)(2,1)} %lat_hbm.1, bf16[32,64,128]{2,1,0:T(8,128)(2,1)} %bitcast.8, bf16[256,128]{1,0:T(8,128)(2,1)} %bitcast.9, bf16[256,64]{1,0:T(8,128)(2,1)} %bitcast.10, ...), custom_call_target="tpu_custom_call" | custom-call | tf_op jit(solution)/shard_map/decode_and_move/pallas_call | solution.py:562
  50.5 2.3 %hand_out.1 = (f32[256,128]{1,0:T(8,128)}, bf16[32,128,512]{2,1,0:T(8,128)(2,1)}, bf16[32,64,128]{2,1,0:T(8,128)(2,1)}) custom-call(f32[256,128]{1,0:T(8,128)S(1)} %get-tuple-element.9.att, bf16[32,128,512]{2,1,0:T(8,128)(2,1)S(1)} %get-tuple-element.10.lat, bf16[8,16,16,128]{3,2,1,0:T(8,128)(2,1)S(1)} %get-tuple-element.11.rope), custom_call_target="tpu_custom_call" | custom-call | tf_op jit(solution)/shard_map/hand_out/pallas_call | solution.py:628
